TPU v7x, 128 devices: a whole 4x4x4 slice. The times are simulated.
128 devices in a mesh: seq: 16 (over z_hi, y, core), kv: 8 (over x, z_lo).
Axes of the slice: x: 4, y: 4, z: 4 (z_hi: 2, z_lo: 2; z = z_hi * 2 + z_lo), core: 2. Of those that a mesh axis runs over, the one named last changes fastest.
Arguments:
- queries: bfloat16 [16384, 4096], P('seq', 'kv'), may hold values from -100 to 100
- resp_keys: bfloat16 [16384, 1024], P('seq', 'kv'), may hold values from -6 to 6
- resp_values: bfloat16 [16384, 1024], P('seq', 'kv'), may hold values from -6 to 6
- prompt_keys: bfloat16 [16384, 1024], P('seq', 'kv'), may hold values from -6 to 6
- prompt_values: bfloat16 [16384, 1024], P('seq', 'kv'), may hold values from -6 to 6
- out_weight: bfloat16 [4096, 4096], P('kv'), may hold values from -0.125 to 0.125
- grad_out: bfloat16 [16384, 4096], P('seq', 'kv'), may hold values from -6 to 6
- response_group: int32 [256, 1], P('seq'), may hold values from 0 to 15
- prompt_len: int32 [16], replicated, may hold values from 256 to 1024, as said below
Outputs:
- layer_out: bfloat16 [16384, 4096], P('seq', 'kv')
- query_grad: bfloat16 [16384, 4096], P('seq', 'kv')
- key_grad: bfloat16 [16384, 1024], P('seq', 'kv')
- value_grad: bfloat16 [16384, 1024], P('seq', 'kv')
- prompt_key_grad: bfloat16 [16384, 1024], P('seq', 'kv')
- prompt_value_grad: bfloat16 [16384, 1024], P('seq', 'kv')
Inputs may be any that keep to these rules, and one draw needn't show every extreme that they name: `prompt_len`: at least one group has all 1024 prompt tokens live. `response_group`: every group has at least one response.
All inputs are finite; a program needn't handle non-finite values.
Results may differ from a plain program's by a relative error of at most 0.04.
Values may be sent and summed in bfloat16 or wider, within the bound.
No kernel may reach another device: no remote copies, remote signals or barrier semaphores. Data moves between devices by JAX's collectives and lax.ppermute only.
A program may use at most 192 MiB of HBM per device.

v0:
```python
import jax
import jax.numpy as jnp
from jax import lax
from jax.sharding import PartitionSpec as P

HD = 128
QPK = 4
PL = 1024
RL = 64


def body(
    queries,
    resp_keys,
    resp_values,
    prompt_keys,
    prompt_values,
    out_weight,
    grad_out,
    response_group,
    prompt_len,
):
    f32 = jnp.float32
    score_scale = HD ** (-0.5)
    slots = response_group.shape[0]
    kv_here = resp_keys.shape[1] // HD
    groups_all = lax.axis_size("seq")
    token_rows = queries.shape[0]
    gathered_keys, gathered_values = (
        lax.all_gather(prompt_keys, "seq", axis=0, tiled=True),
        lax.all_gather(prompt_values, "seq", axis=0, tiled=True),
    )
    groups = response_group[:, 0]
    member = groups[:, None] == jnp.arange(groups_all, dtype=jnp.int32)[None, :]
    prompt_live = jnp.sum(jnp.where(member, prompt_len[None, :], 0), axis=1)
    prompt_k = gathered_keys.reshape(groups_all, PL, kv_here, HD)[groups]
    prompt_v = gathered_values.reshape(groups_all, PL, kv_here, HD)[groups]
    all_keys = jnp.concatenate([prompt_k, resp_keys.reshape(slots, RL, kv_here, HD)], axis=1)
    all_values = jnp.concatenate([prompt_v, resp_values.reshape(slots, RL, kv_here, HD)], axis=1)
    query_blk = queries.reshape(slots, RL, kv_here, QPK, HD)
    scores = (
        jnp.einsum("rihgd,rjhd->rhgij", query_blk, all_keys, preferred_element_type=f32)
        * score_scale
    )
    key_pos = jnp.arange(PL + RL)[None, None, :]
    query_pos = jnp.arange(RL)[None, :, None]
    visible = jnp.where(
        key_pos < PL, key_pos < prompt_live[:, None, None], key_pos - PL <= query_pos
    )
    scores = jnp.where(visible[:, None, None], scores, -jnp.inf)
    row_max = jnp.max(scores, axis=-1, keepdims=True)
    expo = jnp.exp(scores - row_max)
    weights = expo / jnp.sum(expo, axis=-1, keepdims=True)
    weights_bf = weights.astype(jnp.bfloat16)
    attended = jnp.einsum(
        "rhgij,rjhd->rihgd", weights_bf, all_values, preferred_element_type=f32
    ).astype(jnp.bfloat16)
    attended_rows = attended.reshape(token_rows, kv_here * QPK * HD)
    partial_out = jnp.dot(attended_rows, out_weight, preferred_element_type=f32)
    layer_out = lax.psum_scatter(
        partial_out.astype(jnp.bfloat16), "kv", scatter_dimension=1, tiled=True
    )
    attended_grad = jnp.einsum(
        "tn,cn->tc",
        lax.all_gather(grad_out, "kv", axis=1, tiled=True),
        out_weight,
        preferred_element_type=f32,
    ).astype(jnp.bfloat16)
    attended_grad = attended_grad.reshape(slots, RL, kv_here, QPK, HD)
    grad_values = jnp.einsum(
        "rhgij,rihgd->rjhd", weights_bf, attended_grad, preferred_element_type=f32
    )
    prob_grad = jnp.einsum(
        "rihgd,rjhd->rhgij", attended_grad, all_values, preferred_element_type=f32
    )
    row_dot = jnp.sum(attended_grad.astype(f32) * attended.astype(f32), axis=-1)
    row_dot = jnp.transpose(row_dot, (0, 2, 3, 1))[..., None]
    score_grad = (weights * (prob_grad - row_dot)).astype(jnp.bfloat16)
    query_grad = (
        jnp.einsum("rhgij,rjhd->rihgd", score_grad, all_keys, preferred_element_type=f32)
        * score_scale
    ).astype(jnp.bfloat16)
    grad_keys = (
        jnp.einsum("rhgij,rihgd->rjhd", score_grad, query_blk, preferred_element_type=f32)
        * score_scale
    )
    key_grad = grad_keys[:, PL:].astype(jnp.bfloat16).reshape(token_rows, kv_here * HD)
    value_grad = grad_values[:, PL:].astype(jnp.bfloat16).reshape(token_rows, kv_here * HD)
    member_f = member.astype(f32)
    part_k = jnp.einsum(
        "rg,rphd->gphd", member_f, grad_keys[:, :PL], precision=lax.Precision.HIGHEST
    )
    part_v = jnp.einsum(
        "rg,rphd->gphd", member_f, grad_values[:, :PL], precision=lax.Precision.HIGHEST
    )
    part_k = part_k.reshape(groups_all * PL, kv_here * HD)
    part_v = part_v.reshape(groups_all * PL, kv_here * HD)
    summed_k, summed_v = (
        lax.psum_scatter(
            part_k.astype(jnp.bfloat16), "seq", scatter_dimension=0, tiled=True
        ).astype(jnp.float32),
        lax.psum_scatter(
            part_v.astype(jnp.bfloat16), "seq", scatter_dimension=0, tiled=True
        ).astype(jnp.float32),
    )
    prompt_key_grad = summed_k.astype(jnp.bfloat16)
    prompt_value_grad = summed_v.astype(jnp.bfloat16)
    query_grad = query_grad.reshape(token_rows, kv_here * QPK * HD)
    return (layer_out, query_grad, key_grad, value_grad, prompt_key_grad, prompt_value_grad)


def solution(mesh):
    return jax.shard_map(
        body,
        mesh=mesh,
        in_specs=(
            P("seq", "kv"),
            P("seq", "kv"),
            P("seq", "kv"),
            P("seq", "kv"),
            P("seq", "kv"),
            P("kv", None),
            P("seq", "kv"),
            P("seq", None),
            P(),
        ),
        out_specs=(
            P("seq", "kv"),
            P("seq", "kv"),
            P("seq", "kv"),
            P("seq", "kv"),
            P("seq", "kv"),
            P("seq", "kv"),
        ),
        check_vma=False,
    )
```

profile of v0, /device:TPU:1, one launch (start us, length us, event | category | flops | bytes accessed | tf_op | source)
XLA Modules:
  0.0 711.9 jit_solution(6128480140138342456)
XLA Ops:
  12.9 57.3 %all-gather.6.cloned.1.call-done = bf16[16384,128]{1,0:T(8,128)(2,1)} async-done(((bf16[1024,128]{1,0:T(8,128)(2,1)}), bf16[16384,128]{1,0:T(8,128)(2,1)}) %all-gather.6.cloned.1.call-update) | async-done | bytes 4194320 | tf_op jit(solution)/shard_map/all_gather | solution.py:30
  70.2 5.3 gather_fusion.1
  75.5 51.9 %all-gather.4.cloned.1.call-done = bf16[16384,128]{1,0:T(8,128)(2,1)} async-done(((bf16[1024,128]{1,0:T(8,128)(2,1)}), bf16[16384,128]{1,0:T(8,128)(2,1)}) %all-gather.4.cloned.1.call-update) | async-done | bytes 4194320 | tf_op jit(solution)/shard_map/all_gather | solution.py:31
  127.4 5.3 gather_fusion
  132.7 10.0 %fusion.2 = (f32[16,4,64]{2,1,0:T(4,128)S(1)}, f32[16,1088,64,4]{1,2,3,0:T(8,128)}) fusion(pred[16,64,1088]{2,1,0:T(8,128)(4,1)S(1)} %broadcast_select_fusion, bf16[16,64,4,128]{3,2,1,0:T(4,128)(2,1)S(1)} %reshape.187, bf16[16,64,1,128]{3,1,0,2:T(8,128)(2,1)S(1)} %bitcast.161, bf16[16,1024,1,128]{3,1,0,2:T(8,128)(2,1)} %bitcast.145), kind=kOutput, calls=%fused_computation.8 | convolution fusion | flops 1163128832 | bytes 24461312 | tf_op jit(solution)/shard_map/rihgd,rjhd->rhgij/dot_general | solution.py:42
  142.7 8.7 %fusion.4 = f32[16,4,64]{2,1,0:T(4,128)S(1)} fusion(f32[16,1088,64,4]{1,2,3,0:T(8,128)} %get-tuple-element.7, f32[16,4,64]{2,1,0:T(4,128)S(1)} %get-tuple-element.6, pred[16,64,1088]{2,1,0:T(8,128)(4,1)S(1)} %broadcast_select_fusion), kind=kLoop, calls=%fused_computation.10 | loop fusion | flops 13365248 | bytes 18972672 | tf_op jit(solution)/shard_map/reduce_sum | solution.py:53
  151.4 144.3 %all-gather.8.cloned.1.call-done = bf16[1024,4096]{1,0:T(8,128)(2,1)} async-done(((bf16[1024,512]{1,0:T(8,128)(2,1)}), bf16[1024,4096]{1,0:T(8,128)(2,1)}) %all-gather.8.cloned.1.call-update) | async-done | bytes 8388624 | tf_op jit(solution)/shard_map/all_gather | solution.py:65
  295.7 10.1 %convolution_convert_fusion.1 = bf16[1024,512]{1,0:T(8,128)(2,1)} fusion(bf16[1024,4096]{1,0:T(8,128)(2,1)} %all-gather.8.cloned.1.call-done, bf16[512,4096]{1,0:T(8,128)(2,1)} %param.14), kind=kOutput, calls=%fused_computation.36 | convolution fusion | flops 4295491584 | bytes 13631488 | tf_op jit(solution)/shard_map/tn,cn->tc/dot_general | solution.py:63
  305.7 2.7 reshape.197
  310.6 11.4 %fusion.26 = (f32[16,64,4]{1,2,0:T(4,128)S(1)}, bf16[16,64,1,4,128]{4,1,3,0,2:T(8,128)(2,1)}) fusion(f32[16,64,1,4,128]{4,3,1,0,2:T(4,128)} %reshape.197, f32[16,4,64]{2,1,0:T(4,128)S(1)} %fusion.4, f32[16,4,64]{2,1,0:T(4,128)S(1)} %get-tuple-element.6, f32[16,1088,64,4]{1,2,3,0:T(8,128)} %get-tuple-element.7, ...), kind=kOutput, calls=%fused_computation.34 | convolution fusion | flops 1169682432 | bytes 26591232 | tf_op jit(solution)/shard_map/rhgij,rjhd->rihgd/dot_general | solution.py:55
  322.0 13.4 %fusion.5 = bf16[16,4,64,1088]{3,2,1,0:T(8,128)(2,1)} fusion(f32[16,4,64]{2,1,0:T(4,128)S(1)} %bitcast.163, f32[16,4,64]{2,1,0:T(4,128)S(1)} %fusion.4, f32[16,4,64]{2,1,0:T(4,128)S(1)} %get-tuple-element.6, f32[16,1088,64,4]{1,2,3,0:T(8,128)} %get-tuple-element.7, pred[16,64,1088]{2,1,0:T(8,128)(4,1)S(1)} %broadcast_select_fusion, ...), kind=kOutput, calls=%fused_computation.11 | convolution fusion | flops 1176502272 | bytes 33406976 | tf_op jit(solution)/shard_map/rihgd,rjhd->rhgij/dot_general | solution.py:73
  335.4 10.1 %fusion.11 = f32[16,1088,1,128]{3,1,0,2:T(8,128)} fusion(bf16[16,4,64,1088]{3,2,1,0:T(8,128)(2,1)} %fusion.5, bf16[16,64,4,128]{3,2,1,0:T(4,128)(2,1)S(1)} %reshape.187), kind=kOutput, calls=%fused_computation.18 | convolution fusion | flops 1143078912 | bytes 18874368 | tf_op jit(solution)/shard_map/rhgij,rihgd->rjhd/dot_general | solution.py:84
  345.5 4.0 slice_bitcast_fusion.1
  349.5 11.5 %fusion.20 = bf16[16,1024,128]{2,0,1:T(8,128)(2,1)S(1)} fusion(f32[16,1024,128]{2,1,0:T(8,128)S(1)} %slice_bitcast_fusion.1, s32[16]{0:T(128)S(1)} %bitcast.157), kind=kOutput, calls=%fused_computation.30 | convolution fusion | flops 404750592 | bytes 12582976 | tf_op jit(solution)/shard_map/rg,rphd->gphd/dot_general | solution.py:90
  361.0 3.0 copy.29
  364.1 9.9 %fusion.16 = f32[16,1088,1,128]{3,1,0,2:T(8,128)S(1)} fusion(bf16[16,64,4,128]{3,2,1,0:T(4,128)(2,1)S(1)} %copy-done.2, f32[16,4,64]{2,1,0:T(4,128)S(1)} %fusion.4, f32[16,4,64]{2,1,0:T(4,128)S(1)} %get-tuple-element.6, f32[16,1088,64,4]{1,2,3,0:T(8,128)} %get-tuple-element.7, pred[16,64,1088]{2,1,0:T(8,128)(4,1)S(1)} %broadcast_select_fusion), kind=kOutput, calls=%fused_computation.26 | convolution fusion | flops 1158676480 | bytes 28934144 | tf_op jit(solution)/shard_map/rhgij,rihgd->rjhd/dot_general | solution.py:70
  374.8 2.6 copy-done
  377.4 11.5 %fusion.23 = bf16[16,1024,128]{2,0,1:T(8,128)(2,1)S(1)} fusion(f32[16,1024,128]{2,1,0:T(8,128)S(1)} %slice_bitcast_fusion, s32[16]{0:T(128)S(1)} %bitcast.158), kind=kOutput, calls=%fused_computation.31 | convolution fusion | flops 404750592 | bytes 12582976 | tf_op jit(solution)/shard_map/rg,rphd->gphd/dot_general | solution.py:93
  388.9 3.0 copy.31
  392.9 9.1 %convolution_convert_fusion = bf16[1024,4096]{1,0:T(8,128)(2,1)} fusion(bf16[512,4096]{1,0:T(8,128)(2,1)} %param.14, bf16[128,8,4,128]{3,2,1,0:T(4,128)(2,1)S(1)} %bitcast.153), kind=kOutput, calls=%fused_computation.25 | convolution fusion | flops 4299161600 | bytes 13631488 | tf_op jit(solution)/shard_map/dot_general | solution.py:59
  405.8 7.5 %fusion.33 = bf16[16,64,1,4,128]{4,1,3,0,2:T(8,128)(2,1)S(1)} fusion(bf16[16,4,64,1088]{3,2,1,0:T(8,128)(2,1)} %fusion.5, bf16[16,64,1,128]{3,1,0,2:T(8,128)(2,1)S(1)} %bitcast.162, bf16[16,1024,1,128]{3,1,0,2:T(8,128)(2,1)} %bitcast.146), kind=kOutput, calls=%fused_computation.39 | convolution fusion | flops 1150812160 | bytes 14417920 | tf_op jit(solution)/shard_map/rhgij,rjhd->rihgd/dot_general | solution.py:80
  415.4 33.1 %reduce-scatter.6.cloned.1.call-done = bf16[1024,128]{1,0:T(8,128)(2,1)} async-done(((bf16[16384,128]{1,0:T(8,128)(2,1)}), bf16[1024,128]{1,0:T(8,128)(2,1)}) %reduce-scatter.6.cloned.1.call-update) | async-done | bytes 262160 | tf_op jit(solution)/shard_map/reduce_scatter | solution.py:99
  448.6 84.0 %reduce-scatter.8.cloned.1.call-done = bf16[1024,128]{1,0:T(8,128)(2,1)} async-done(((bf16[16384,128]{1,0:T(8,128)(2,1)}), bf16[1024,128]{1,0:T(8,128)(2,1)}) %reduce-scatter.8.cloned.1.call-update) | async-done | bytes 262160 | tf_op jit(solution)/shard_map/reduce_scatter | solution.py:102
  532.6 172.0 %reduce-scatter.4.cloned.1.call-done = bf16[1024,512]{1,0:T(8,128)(2,1)} async-done(((bf16[1024,4096]{1,0:T(8,128)(2,1)}), bf16[1024,512]{1,0:T(8,128)(2,1)}) %reduce-scatter.4.cloned.1.call-update) | async-done | bytes 1048592 | tf_op jit(solution)/shard_map/reduce_scatter | solution.py:60
  (39 shorter events, 15.4 us)
Async XLA Ops:
  7.2 63.0 %all-gather.6.cloned.1.call-start = ((), (), s32[]{:S(2)}) async-start(), calls=%async_computation.4 | async-start | bytes 4456448 | tf_op jit(solution)/shard_map/all_gather | solution.py:30
  7.9 119.5 %all-gather.4.cloned.1.call-start = ((), (), s32[]{:S(2)}) async-start(), calls=%async_computation.3 | async-start | bytes 4456448 | tf_op jit(solution)/shard_map/all_gather | solution.py:31
  8.6 287.0 %all-gather.8.cloned.1.call-start = ((), (), s32[]{:S(2)}) async-start(), calls=%async_computation.6 | async-start | bytes 9437184 | tf_op jit(solution)/shard_map/all_gather | solution.py:65
  9.4 439.2 %reduce-scatter.6.cloned.1.call-start = ((), (), s32[]{:S(2)}) async-start(), calls=%async_computation.7 | async-start | bytes 4456448 | tf_op jit(solution)/shard_map/reduce_scatter | solution.py:99
  70.2 62.5 %copy-start.5 = (bf16[1024,128]{1,0:T(8,128)(2,1)S(1)}, bf16[1024,128]{1,0:T(8,128)(2,1)}, u32[]{:S(2)}) copy-start(bf16[1024,128]{1,0:T(8,128)(2,1)} %param.10) | copy-start | bytes 786436
  151.4 159.1 %copy-start.4 = (bf16[1024,128]{1,0:T(8,128)(2,1)S(1)}, bf16[1024,128]{1,0:T(8,128)(2,1)}, u32[]{:S(2)}) copy-start(bf16[1024,128]{1,0:T(8,128)(2,1)} %param.11) | copy-start | bytes 786436
  345.5 4.0 copy-start.3
  361.0 3.1 copy-start.2
  364.0 168.6 %reduce-scatter.8.cloned.1.call-start = ((), (), s32[]{:S(2)}) async-start(), calls=%async_computation.8 | async-start | bytes 4456448 | tf_op jit(solution)/shard_map/reduce_scatter | solution.py:102
  374.0 3.4 copy-start
  388.9 3.1 copy-start.1
  392.0 312.6 %reduce-scatter.4.cloned.1.call-start = ((), (), s32[]{:S(2)}) async-start(), calls=%async_computation.5 | async-start | bytes 9437184 | tf_op jit(solution)/shard_map/reduce_scatter | solution.py:60
Sparse Core Ops, SparseCore 0:
  10.4 59.7 all-gather.5
  72.7 54.7 all-gather.3
  129.1 166.5 all-gather.7
  364.1 84.3 reduce-scatter.5
  453.6 78.9 reduce-scatter.7
  535.4 169.1 reduce-scatter.3
where the time goes:
time: 721 us; the launch traced here: 712 us
  waiting for transfers between devices  545 us (76%)
  matrix products  105 us (15%)
  local copies, waits for them, and re-layouts  36.9 us (5%)
  between operations  14.7 us (2%)
  other arithmetic  10.8 us (1%)
    reduce_scatter x1, waiting for transfers between devices, body(): lax.psum_scatter(partial_out.astype(jnp.bfloat16), 'kv', scatter_dimensio...  172 us
    all_gather x1, waiting for transfers between devices, body(): lax.all_gather(grad_out, 'kv', axis=1, tiled=True)  144 us
    reduce_scatter x1, waiting for transfers between devices, body(): lax.psum_scatter(part_v.astype(jnp.bfloat16), 'seq', scatter_dimension=0,...  84 us
    all_gather x1, waiting for transfers between devices, body(): lax.all_gather(prompt_keys, 'seq', axis=0, tiled=True)  57.3 us
    all_gather x1, waiting for transfers between devices, body(): lax.all_gather(prompt_values, 'seq', axis=0, tiled=True)  51.9 us
    reduce_scatter x1, waiting for transfers between devices, body(): lax.psum_scatter(part_k.astype(jnp.bfloat16), 'seq', scatter_dimension=0,...  33.1 us
  transfers between devices with their start and end apart: 6, of which 6 were waited for; matrix products, arithmetic and copies ran while one was open for 11% of the time, Pallas kernels for 0%

commit v1 on v0

v1 whole, which is shorter than its diff:
```python
import functools
import math

import jax
import jax.numpy as jnp
from jax import lax
from jax.experimental import pallas as pl
from jax.experimental.pallas import tpu as pltpu
from jax.sharding import PartitionSpec as P

HD = 128
QPK = 4
PL = 1024
RL = 64
ROWS = QPK * RL
TILE = 256
NT = PL // TILE
SCALE = HD ** (-0.5)
LOG2E = math.log2(math.e)
C2 = SCALE * LOG2E
MIB = 1024 * 1024
F32 = jnp.float32
BF16 = jnp.bfloat16

SIDE = 8
KV_BUFS = 3


def kv_perm(move):
    return [
        (x * 2 + z, (move(x, z)[0] % 4) * 2 + move(x, z)[1]) for x in range(4) for z in range(2)
    ]


def seq_perm(move):
    pairs = []
    for h in range(2):
        for y in range(4):
            for c in range(2):
                h2, y2, c2 = move(h, y, c)
                pairs.append((h * 8 + y * 2 + c, h2 * 8 + (y2 % 4) * 2 + c2))
    return pairs


X_UP = kv_perm(lambda x, z: (x + 1, z))
X_DOWN = kv_perm(lambda x, z: (x - 1, z))
Z_LO = kv_perm(lambda x, z: (x, 1 - z))
Z_HI = seq_perm(lambda h, y, c: (1 - h, y, c))
CORE = seq_perm(lambda h, y, c: (h, y, 1 - c))
SIDE_GROUPS = [[h * SIDE + i for i in range(SIDE)] for h in range(2)]
Y_UP = seq_perm(lambda h, y, c: (h, y + 1, c))
Y_DOWN = seq_perm(lambda h, y, c: (h, y - 1, c))


def kv_send(a, perm):
    return lax.ppermute(a, "kv", perm)


def seq_send(a, perm):
    return lax.ppermute(a, "seq", perm)


def dot_nt(a, b):
    return lax.dot_general(a, b, (((1,), (1,)), ((), ())), preferred_element_type=F32)


def dot_nn(a, b):
    return lax.dot_general(a, b, (((1,), (0,)), ((), ())), preferred_element_type=F32)


def dot_tn(a, b):
    return lax.dot_general(a, b, (((0,), (0,)), ((), ())), preferred_element_type=F32)


def stacked_heads(block):
    return jnp.concatenate([block[:, h * HD : (h + 1) * HD] for h in range(QPK)], axis=0)


def spread_heads(stacked):
    return jnp.concatenate([stacked[h * RL : (h + 1) * RL] for h in range(QPK)], axis=1)


def causal_mask():
    key = lax.broadcasted_iota(jnp.int32, (RL, ROWS), 0)
    query = lax.broadcasted_iota(jnp.int32, (RL, ROWS), 1) % RL
    return key <= query


def tile_mask(tile, live):
    key = lax.broadcasted_iota(jnp.int32, (TILE, ROWS), 0) + tile * TILE
    return key < live


ANY = pl.BlockSpec(memory_space=pl.ANY)
SMEM = pl.BlockSpec(memory_space=pltpu.SMEM)
VMEM = pl.BlockSpec(memory_space=pltpu.VMEM)


def work_of(us):
    return pl.CostEstimate(flops=int(us * 1.15e9), bytes_accessed=int(us * 1e5), transcendentals=0)


def run(kernel, scalars, near, far, after, outs, scratch, mib, name, cost, out_specs=None, aliases=None):
    n_in, n_after = len(scalars) + len(near) + len(far), len(after)

    def entry(*refs):
        kernel(*refs[:n_in], *refs[n_in + n_after :])

    return pl.pallas_call(
        entry,
        out_shape=tuple(outs),
        in_specs=[SMEM] * len(scalars) + [VMEM] * len(near) + [ANY] * (len(far) + n_after),
        out_specs=out_specs or (ANY,) * len(outs),
        scratch_shapes=scratch,
        input_output_aliases=aliases or {},
        compiler_params=pltpu.CompilerParams(vmem_limit_bytes=mib * MIB),
        cost_estimate=work_of(cost),
        name=name,
    )(*scalars, *near, *far, *after)


def copy_all(pairs, sems, rows=256):
    for i, (src, dst) in enumerate(pairs):
        for lo in range(0, src.shape[0], rows):
            piece = pl.ds(lo, min(rows, src.shape[0]))
            pltpu.make_async_copy(src.at[piece], dst.at[piece], sems.at[i]).start()
    return [pltpu.make_async_copy(src, dst, sems.at[i]) for i, (src, dst) in enumerate(pairs)]


def place_of(at, slot):
    return lax.rem(at[3] + lax.rem(slot, 4), 4) * 2 + (at[2] ^ (1 - slot // 4))


def prompt_rows(place):
    return pl.ds(pl.multiple_of(place * PL, PL), PL)


def start_slot(at, kv_in, starts, slot, last, kv_buf, sem):
    known = lax.min(slot, last - 1)

    @pl.when((slot < last) & (starts[known + 1] > starts[known]))
    def _():
        buf = lax.rem(slot, KV_BUFS)
        pltpu.make_async_copy(kv_in.at[prompt_rows(place_of(at, slot))], kv_buf.at[buf], sem.at[buf]).start()


def wait_slot(kv_in, buf, kv_buf, sem):
    pltpu.make_async_copy(kv_in.at[pl.ds(0, PL)], kv_buf.at[buf], sem.at[buf]).wait()


def per_response(order, lives, starts, slot, work):
    def one(p, carry):
        r = order[p]
        live = lives[p]
        tiles = (live + TILE - 1) // TILE
        row = pl.ds(pl.multiple_of(r * RL, RL), RL)
        for n in range(1, NT + 1):
            pl.when(tiles == n)(functools.partial(work, r, row, live, n))
        return carry

    lax.fori_loop(starts[slot], starts[slot + 1], one, 0)


def lse_rows(r):
    return pl.ds(pl.multiple_of(r * 8, 8), 8)


def load_all(pairs, sems):
    for c in copy_all(pairs, sems, 256):
        c.wait()


def fwd_kernel(at, starts, order, lives, q_in, k_in, v_in, *rest):
    kv_in, att_ref, lse_ref, q_ref, k_ref, v_ref, kv_buf, kv_sem, in_sem = rest[-9:]
    earlier = rest[:-9]
    for i in range(KV_BUFS - 1):
        start_slot(at, kv_in, starts, i, SIDE, kv_buf, kv_sem)
    local = ((q_in, q_ref), (k_in, k_ref), (v_in, v_ref))
    for c in copy_all([*local, *zip(earlier, (att_ref, lse_ref))], in_sem, 128):
        c.wait()

    def one_slot(slot, carry):
        kv = lax.rem(slot, KV_BUFS)
        start_slot(at, kv_in, starts, slot + KV_BUFS - 1, SIDE, kv_buf, kv_sem)

        @pl.when(starts[slot + 1] > starts[slot])
        def _():
            wait_slot(kv_in, kv, kv_buf, kv_sem)

        def work(r, row, live, n):
            q = stacked_heads(q_ref[row, :])
            scores = [dot_nt(kv_buf[kv, t * TILE : (t + 1) * TILE, :HD], q) for t in range(n)]
            scores[-1] = jnp.where(tile_mask(n - 1, live), scores[-1], -jnp.inf)
            own = jnp.where(causal_mask(), dot_nt(k_ref[row, :], q), -jnp.inf)
            top = jnp.max(own, axis=0, keepdims=True)
            for s in scores:
                top = jnp.maximum(top, jnp.max(s, axis=0, keepdims=True))
            top = top * C2
            w_own = jnp.exp2(own * C2 - top)
            total = jnp.sum(w_own, axis=0, keepdims=True)
            out = dot_tn(v_ref[row, :], w_own.astype(BF16))
            for t, s in enumerate(scores):
                w = jnp.exp2(s * C2 - top)
                total = total + jnp.sum(w, axis=0, keepdims=True)
                out = out + dot_tn(kv_buf[kv, t * TILE : (t + 1) * TILE, HD:], w.astype(BF16))
            out = out * (1.0 / total)
            att_ref[row, :] = spread_heads(out.T.astype(BF16))
            lse_ref[lse_rows(r), :] = jnp.broadcast_to(top + jnp.log2(total), (8, ROWS))

        per_response(order, lives, starts, slot, work)
        return carry

    lax.fori_loop(0, SIDE, one_slot, 0)


def bwd_kernel(slots, whole, at, starts, order, lives, *refs):
    ins, (dq_ref, dk_ref, dv_ref, sum_ref), scratch = refs[: -4 - 16], refs[-4 - 16 : -16], refs[-16:]
    q_in, k_in, v_in, att_in, lse_in, own_in, got_in, kv_in, *earlier = ins
    q_ref, k_ref, v_ref, att_ref, lse_ref, own_s, got_s, dq_s, dk_s, dv_s, kv_buf, k_t, acc, blk_s, kv_sem, in_sem = scratch
    first, last = slots
    for i in range(first, first + KV_BUFS - 1):
        start_slot(at, kv_in, starts, i, last, kv_buf, kv_sem)
    local = (
        (q_in, q_ref), (k_in, k_ref), (v_in, v_ref), (att_in, att_ref), (lse_in, lse_ref), (own_in, own_s),
        (got_in, got_s),
    )
    for c in copy_all([*local, *zip(earlier, (dq_s, dk_s, dv_s))], in_sem, 256):
        c.wait()

    def put(slot):
        blk = lax.rem(slot, 2)
        place = place_of(at, slot) if whole else slot - first
        return pltpu.make_async_copy(blk_s.at[blk], sum_ref.at[prompt_rows(place)], in_sem.at[blk])

    def one_slot(slot, carry):
        kv = lax.rem(slot, KV_BUFS)
        start_slot(at, kv_in, starts, slot + KV_BUFS - 1, last, kv_buf, kv_sem)
        acc[...] = jnp.zeros_like(acc)

        @pl.when(starts[slot + 1] > starts[slot])
        def _():
            wait_slot(kv_in, kv, kv_buf, kv_sem)
            k_t[...] = kv_buf[kv, :, :HD].T

        def work(r, row, live, n):
            q = stacked_heads(q_ref[row, :])
            got = got_s[row, :]
            low, high = got[:, : 2 * HD], got[:, 2 * HD :]
            got = jnp.concatenate([jnp.where(at[2] == 0, low, high), jnp.where(at[2] == 0, high, low)], axis=1)
            da = (stacked_heads(own_s[row, :]).astype(F32) + stacked_heads(got).astype(F32)).astype(BF16)
            prod = da.astype(F32) * stacked_heads(att_ref[row, :]).astype(F32)
            near = prod.astype(BF16)
            rest_of = (prod - near.astype(F32)).astype(BF16)
            ones = jnp.ones((8, HD), BF16)
            row_dot = (dot_nt(ones, near) + dot_nt(ones, rest_of))[:1]
            lse = lse_ref[lse_rows(r), :][:1]
            k_own = k_ref[row, :]
            w = jnp.exp2(dot_nt(k_own, q) * C2 - lse)
            w = jnp.where(causal_mask(), w, 0.0)
            ds = (w * (dot_nt(v_ref[row, :], da) - row_dot)).astype(BF16)
            dk_s[row, :] = (dot_nn(ds, q) * SCALE).astype(BF16)
            dv_s[row, :] = dot_nn(w.astype(BF16), da).astype(BF16)
            dq = dot_tn(k_own, ds)
            for t in range(n):
                span = slice(t * TILE, (t + 1) * TILE)
                s = dot_nt(kv_buf[kv, span, :HD], q)
                w = jnp.exp2(s * C2 - lse)
                if t == n - 1:
                    w = jnp.where(tile_mask(t, live), w, 0.0)
                ds = (w * (dot_nt(kv_buf[kv, span, HD:], da) - row_dot)).astype(BF16)
                acc[span, :HD] += dot_nn(ds, q)
                acc[span, HD:] += dot_nn(w.astype(BF16), da)
                dq = dq + dot_nn(k_t[:, span], ds)
            dq_s[row, :] = spread_heads((dq * SCALE).T.astype(BF16))

        per_response(order, lives, starts, slot, work)

        @pl.when(slot >= first + 2)
        def _():
            put(slot - 2).wait()

        blk = lax.rem(slot, 2)
        blk_s[blk, :, :HD] = (acc[:, :HD] * SCALE).astype(BF16)
        blk_s[blk, :, HD:] = acc[:, HD:].astype(BF16)
        put(slot).start()
        return carry

    lax.fori_loop(first, last, one_slot, 0)
    put(jnp.int32(last - 2)).wait()
    put(jnp.int32(last - 1)).wait()
    for c in copy_all(((dq_s, dq_ref), (dk_s, dk_ref), (dv_s, dv_ref)), in_sem, 256):
        c.wait()


def shape(*dims, dtype=BF16):
    return jax.ShapeDtypeStruct(dims, dtype)


def attention_fwd(at, starts, order, lives, q, k, v, kv, earlier, after):
    return run(
        fwd_kernel,
        (at, starts, order, lives),
        (),
        (q, k, v, *earlier, kv),
        after,
        (shape(*q.shape), shape(q.shape[0] // RL * 8, ROWS, dtype=F32)),
        [
            pltpu.VMEM(q.shape, BF16),
            pltpu.VMEM(k.shape, BF16),
            pltpu.VMEM(v.shape, BF16),
            pltpu.VMEM((KV_BUFS, PL, 2 * HD), BF16),
            pltpu.SemaphoreType.DMA((KV_BUFS,)),
            pltpu.SemaphoreType.DMA((5,)),
        ],
        56,
        "attention_fwd",
        300,
        (VMEM, VMEM),
    )


def attention_bwd(slots, cost, at, starts, order, lives, q, k, v, att, lse, own, got, kv, earlier, after):
    whole = slots == (0, SIDE)
    return run(
        functools.partial(bwd_kernel, slots, whole),
        (at, starts, order, lives),
        (),
        (q, k, v, att, lse, own, got, kv, *earlier),
        after,
        (shape(*q.shape), shape(*k.shape), shape(*v.shape), shape((slots[1] - slots[0]) * PL, 2 * HD)),
        [
            pltpu.VMEM(q.shape, BF16),
            pltpu.VMEM(k.shape, BF16),
            pltpu.VMEM(v.shape, BF16),
            pltpu.VMEM(q.shape, BF16),
            pltpu.VMEM(lse.shape, F32),
            pltpu.VMEM(q.shape, BF16),
            pltpu.VMEM(q.shape, BF16),
            pltpu.VMEM(q.shape, BF16),
            pltpu.VMEM(k.shape, BF16),
            pltpu.VMEM(v.shape, BF16),
            pltpu.VMEM((KV_BUFS, PL, 2 * HD), BF16),
            pltpu.VMEM((HD, PL), BF16),
            pltpu.VMEM((PL, 2 * HD), F32),
            pltpu.VMEM((2, PL, 2 * HD), BF16),
            pltpu.SemaphoreType.DMA((KV_BUFS,)),
            pltpu.SemaphoreType.DMA((10,)),
        ],
        56,
        "attention_bwd",
        cost,
    )


def weight_column(at, k, z_lo):
    return pl.multiple_of((lax.rem(at[0] + k, 4) * 2 + z_lo) * 512, 512)


def hold(a, after):
    def kernel(a_ref, out):
        pass

    return run(kernel, (), (), (a,), after, (shape(*a.shape),), [], 4, "hold", 0.2, aliases={0: 0})[0]


def pack_prompts(k, v):
    def kernel(k_ref, v_ref, kv_out, kv_s, sems):
        loads = copy_all(((k_ref, kv_s.at[:, pl.ds(0, HD)]), (v_ref, kv_s.at[:, pl.ds(HD, HD)])), sems)
        for c in loads:
            c.wait()
        for c in copy_all(((kv_s, kv_out),), sems):
            c.wait()

    wide = (k.shape[0], 2 * HD)
    return run(
        kernel, (), (), (k, v), (), (shape(*wide),), [pltpu.VMEM(wide, BF16), pltpu.SemaphoreType.DMA((2,))], 56,
        "pack_prompts", 2,
    )[0]


def pack_weight(at, weight, after):
    def kernel(at, w_ref, own, give, own_s, give_s, sems):
        rows = pl.ds(pl.multiple_of(at[2] * 256, 256), 256)
        pairs = []
        for k in range(4):
            cols = pl.ds(k * 512, 512)
            pairs.append((w_ref.at[rows, pl.ds(weight_column(at, k, 1 - at[1]), 512)], give_s.at[:, cols]))
            pairs.append((w_ref.at[:, pl.ds(weight_column(at, k, at[1]), 512)], own_s.at[:, cols]))
        loads = copy_all(pairs, sems)
        for c in loads[0::2]:
            c.wait()
        last = copy_all(((give_s, give),), sems, 64)
        for c in loads[1::2]:
            c.wait()
        for c in last + copy_all(((own_s, own),), sems.at[pl.ds(1, 1)], 128):
            c.wait()

    return run(
        kernel, (at,), (), (weight,), after, (shape(512, 2048), shape(256, 2048)),
        [pltpu.VMEM((512, 2048), BF16), pltpu.VMEM((256, 2048), BF16), pltpu.SemaphoreType.DMA((8,))], 48,
        "pack_weight", 3,
    )


TOKENS = 256


def weight_specs():
    parts = []
    for rows in (512, 256, 256):
        for k in range(4):
            parts.append(pl.BlockSpec((rows, 512), functools.partial(lambda k, i: (0, k), k)))
    return parts


def token_spec(index=lambda i: i):
    return pl.BlockSpec((TOKENS, 512), lambda i: (index(i), 0))


def project(kernel, name, at, arrays, specs, weights, n_out, rows):
    w_own, got_a, got_b = weights
    return pl.pallas_call(
        kernel,
        grid=(rows // TOKENS,),
        out_shape=(shape(rows, 512),) * n_out,
        in_specs=[SMEM, *specs, *weight_specs()],
        out_specs=(token_spec(),) * n_out,
        compiler_params=pltpu.CompilerParams(vmem_limit_bytes=56 * MIB),
        cost_estimate=work_of(0.01),
        name=name,
    )(at, *arrays, *[w_own] * 4, *[got_a] * 4, *[got_b] * 4)


def grad_proj(at, weights, g0, g1, g2_low, g2_high, g3):
    rows = g0.shape[0]
    cut = rows // 2 // TOKENS

    def kernel(at, g0, g1, g2_low, g2_high, g3, *refs):
        w_own, w_a, w_b, (own_ref, other_ref) = refs[:4], refs[4:8], refs[8:12], refs[12:]
        g2 = jnp.where(pl.program_id(0) < cut, g2_low[...], g2_high[...])
        tokens = (g0[...], g1[...], g2, g3[...])
        for w, out, cols in ((w_a, other_ref, slice(0, 256)), (w_b, other_ref, slice(256, 512)), (w_own, own_ref, slice(0, 512))):
            total = None
            for k in range(4):
                part = dot_nt(tokens[k], w[k][...])
                total = part if total is None else total + part
            out[:, cols] = total.astype(BF16)

    low, high = token_spec(lambda i: jnp.minimum(i, cut - 1)), token_spec(lambda i: jnp.maximum(i - cut, 0))
    specs = [token_spec(), token_spec(), low, high, token_spec()]
    return project(kernel, "grad_projection", at, (g0, g1, g2_low, g2_high, g3), specs, weights, 2, rows)


def out_proj(at, weights, att, att_other):
    def kernel(at, att, other, *refs):
        w_own, w_a, w_b, outs = refs[:4], refs[4:8], refs[8:12], refs[12:]
        halves = [other[:, pl.ds(pl.multiple_of(lax.rem(at[2] + i, 2) * 256, 256), 256)] for i in range(2)]
        for k in (2, 3, 1, 0):
            total = dot_nn(att[...], w_own[k][...]) + dot_nn(halves[0], w_a[k][...]) + dot_nn(halves[1], w_b[k][...])
            outs[k][...] = total.astype(BF16)

    specs = [token_spec(), token_spec()]
    return project(kernel, "out_projection", at, (att, att_other), specs, weights, 4, att.shape[0])


def add(*arrays):
    return functools.reduce(lambda a, b: a + b, [a.astype(F32) for a in arrays]).astype(BF16)


def body(
    queries,
    resp_keys,
    resp_values,
    prompt_keys,
    prompt_values,
    out_weight,
    grad_out,
    response_group,
    prompt_len,
):
    kv_at, seq_at = lax.axis_index("kv"), lax.axis_index("seq")
    x, z_lo = kv_at // 2, kv_at % 2
    z_hi, y, core = seq_at // SIDE, (seq_at // 2) % 4, seq_at % 2
    n_resp = response_group.shape[0]

    groups = response_group[:, 0]
    count = jnp.arange(n_resp, dtype=jnp.int32)
    member = groups[:, None] == jnp.arange(2 * SIDE, dtype=jnp.int32)[None, :]
    lives = jnp.sum(jnp.where(member, prompt_len[None, :], 0), axis=1)
    slots = (groups % 2 == core) * 4 + (groups % SIDE // 2 - y) % 4
    ranks = slots + jnp.where(groups // SIDE == z_hi, SIDE, 0)
    sort_key = ranks * n_resp + count
    position = jnp.sum((sort_key[None, :] < sort_key[:, None]).astype(jnp.int32), axis=1)
    placed = position[None, :] == count[:, None]
    order = jnp.sum(jnp.where(placed, count[None, :], 0), axis=1)
    lives_sorted = jnp.sum(jnp.where(placed, lives[None, :], 0), axis=1)
    bounds = jnp.arange(2 * SIDE + 1, dtype=jnp.int32)
    starts = jnp.sum((ranks[None, :] < bounds[:, None]).astype(jnp.int32), axis=1)
    at = jnp.stack([x, z_lo, core, y]).astype(jnp.int32)

    def spread(a):
        return lax.all_gather(a, "seq", axis=0, tiled=True, axis_index_groups=SIDE_GROUPS)

    cut = grad_out.shape[0] // 2
    local = (queries, resp_keys, resp_values)
    responses = (order, lives_sorted, *local)
    kv_own = pack_prompts(prompt_keys, prompt_values)
    kv_near = spread(kv_own)
    kv_other = seq_send(kv_own, Z_HI)
    g3, g1 = kv_send(grad_out, X_UP), kv_send(grad_out, X_DOWN)
    w_own, give = pack_weight(at, out_weight, (kv_own,))
    got_a = kv_send(give, Z_LO)
    g2_low, g2_high = kv_send(g3[:cut], X_UP), kv_send(g1[cut:], X_DOWN)
    got_b = seq_send(got_a, CORE)
    weights = (w_own, got_a, got_b)

    far_starts, near_starts = starts[: SIDE + 1], starts[SIDE:]
    first = attention_fwd(at, near_starts, *responses, kv_near, (), ())
    kv_far = spread(hold(kv_other, (first[1], g2_low, g2_high, got_a)))
    own, other = grad_proj(at, weights, grad_out, g1, hold(g2_low, (first[1],)), g2_high, g3)
    da = (own, kv_send(other, Z_LO))
    att, lse = attention_fwd(at, far_starts, *responses, kv_far, first, (other,))
    att_other = kv_send(att, Z_LO)

    heads = (*responses, att, lse, *da)
    half = SIDE // 2
    *grads, part = attention_bwd((0, SIDE), 15, at, far_starts, *heads, kv_far, (), ())
    from_hi = seq_send(
        lax.psum_scatter(part, "seq", scatter_dimension=0, tiled=True, axis_index_groups=SIDE_GROUPS), Z_HI
    )
    *grads, part = attention_bwd((0, half), 0.01, at, near_starts, *heads, kv_near, grads, (part,))
    got = seq_send(part, CORE)
    o0, o1, o2, o3 = out_proj(at, weights, att, hold(att_other, (part,)))
    far_up, far_down = kv_send(o2[:cut], X_UP), kv_send(o2[cut:], X_DOWN)
    *grads, mine = attention_bwd((half, SIDE), 300, at, near_starts, *heads, kv_near, grads, (o3,))

    def block(n, lo, hi):
        rows = slice(n * PL + lo, n * PL + hi)
        return mine[rows].astype(F32) + got[rows].astype(F32)

    mid = PL // 2
    y_up = seq_send(hold(block(2, 0, mid).astype(BF16), (far_up, far_down)), Y_UP)
    y_down = seq_send(block(2, mid, PL).astype(BF16), Y_DOWN)
    x_down = kv_send(jnp.concatenate([add(o1[:cut], far_up), o1[cut:]], axis=0), X_UP)
    x_up = kv_send(jnp.concatenate([o3[:cut], add(o3[cut:], far_down)], axis=0), X_DOWN)
    from_down = seq_send(jnp.concatenate([add(block(1, 0, mid), y_up), block(1, mid, PL).astype(BF16)], axis=0), Y_UP)
    from_up = seq_send(jnp.concatenate([block(3, 0, mid).astype(BF16), add(block(3, mid, PL), y_down)], axis=0), Y_DOWN)
    layer_out = add(o0, x_up, x_down)
    prompt_grad = add(block(0, 0, PL), from_up, from_down, from_hi)
    return (layer_out, *grads, prompt_grad[:, :HD], prompt_grad[:, HD:])


def solution(mesh):
    return jax.shard_map(
        body,
        mesh=mesh,
        in_specs=(
            P("seq", "kv"),
            P("seq", "kv"),
            P("seq", "kv"),
            P("seq", "kv"),
            P("seq", "kv"),
            P("kv", None),
            P("seq", "kv"),
            P("seq", None),
            P(),
        ),
        out_specs=(
            P("seq", "kv"),
            P("seq", "kv"),
            P("seq", "kv"),
            P("seq", "kv"),
            P("seq", "kv"),
            P("seq", "kv"),
        ),
        check_vma=False,
    )
```

time: 721 us -> 217 us (0.30)
  waiting for transfers between devices: 545 us -> 53.3 us
  matrix products: 105 us -> 0 us
  Pallas kernels: 0 us -> 91.9 us
  starting transfers between devices: 0.24 us -> 28.4 us
  local copies, waits for them, and re-layouts: 36.9 us -> 13.2 us
    reduce_scatter x3 -> x1, waiting for transfers between devices: 289 us -> 0.01 us  [body(): lax.psum_scatter(part, 'seq', scatter_dimension=0, tiled=True, axis_index...]
    all_gather x3 -> x2, waiting for transfers between devices: 253 us -> 20.5 us  [spread(): lax.all_gather(a, 'seq', axis=0, tiled=True, axis_index_groups=SIDE_GROUPS)]
    dot_general x10 -> x0, matrix products: 105 us -> none  [the longest x1 13.4 us: body(): jnp.einsum('rihgd,rjhd->rhgij', attended_grad, all_values, preferred_elem...]
    pallas_call x0 -> x13, Pallas kernels: none -> 91.9 us  [the longest x11 74.6 us: run(): pl.pallas_call(entry, out_shape=tuple(outs), in_specs=[SMEM] * len(scalar...]
    ppermute x0 -> x19, waiting for transfers between devices: none -> 32.8 us  [the longest x11 19.9 us: kv_send(): return lax.ppermute(a, 'kv', perm)]
    ppermute x0 -> x19, starting transfers between devices: none -> 28.2 us  [the longest x8 14.2 us: seq_send(): return lax.ppermute(a, 'seq', perm)]
    gather x2 -> x0, local copies, waits for them, and re-layouts: 10.6 us -> none  [the longest x1 5.3 us: body(): prompt_v = gathered_values.reshape(groups_all, PL, kv_here, HD)[groups]]
    convert_element_type x5 -> x0, local copies, waits for them, and re-layouts: 10.5 us -> none  [the longest x1 3.04 us: body(): part_v.astype(jnp.bfloat16)]
  transfers between devices with their start and end apart: 6 -> 22, of which waited for: 6 -> 9; matrix products, arithmetic and copies ran while one was open for 11% -> 8% of each run, Pallas kernels for 0% -> 42%
where the time goes in v1:
time: 217 us; the launch traced here: 215 us
  Pallas kernels  91.9 us (42%)
  waiting for transfers between devices  53.3 us (25%)
  starting transfers between devices  28.4 us (13%)
  other arithmetic  14 us (6%)
  between operations  14 us (6%)
  local copies, waits for them, and re-layouts  13.2 us (6%)
    pallas_call x11, Pallas kernels, run(): pl.pallas_call(entry, out_shape=tuple(outs), in_specs=[SMEM] * len(scalar...  74.6 us
    all_gather x2, waiting for transfers between devices, spread(): lax.all_gather(a, 'seq', axis=0, tiled=True, axis_index_groups=SIDE_GROUPS)  20.5 us
    ppermute x11, waiting for transfers between devices, kv_send(): return lax.ppermute(a, 'kv', perm)  19.9 us
    pallas_call x2, Pallas kernels, project(): pl.pallas_call(kernel, grid=(rows // TOKENS,), out_shape=(shape(rows, 512...  17.3 us
    ppermute x8, starting transfers between devices, seq_send(): return lax.ppermute(a, 'seq', perm)  14.2 us
    ppermute x11, starting transfers between devices, kv_send(): return lax.ppermute(a, 'kv', perm)  14.1 us
    ppermute x8, waiting for transfers between devices, seq_send(): return lax.ppermute(a, 'seq', perm)  12.9 us
    convert_element_type x5, other arithmetic, add(): functools.reduce(lambda a, b: a + b, [a.astype(F32) for a in arrays])  8.73 us
  transfers between devices with their start and end apart: 22, of which 9 were waited for; matrix products, arithmetic and copies ran while one was open for 8% of the time, Pallas kernels for 42%

profile of v1, /device:TPU:1, one launch (start us, length us, event | category | flops | bytes accessed | tf_op | source)
XLA Modules:
  0.0 214.8 jit_solution(476982873778203492)
XLA Ops:
  9.3 4.5 %collective-permute-start = (bf16[1024,256]{1,0:T(8,128)(2,1)}, bf16[1024,256]{1,0:T(8,128)(2,1)}, u32[]{:S(2)}, u32[]{:S(2)}) collective-permute-start(bf16[1024,256]{1,0:T(8,128)(2,1)} %pack_prompts.1.refs_2_), channel_id=1, source_target_pairs={{0,64},{8,72},{16,80},{24,88},{32,96},{40,104},{48,112},{56,120},{... | collective-permute-start | bytes 1572872 | tf_op jit(solution)/shard_map/ppermute | solution.py:60
  17.6 3.3 %pack_weight.1 = (bf16[512,2048]{1,0:T(8,128)(2,1)S(1)}, bf16[256,2048]{1,0:T(8,128)(2,1)}) custom-call(s32[4]{0:T(128)S(1)} %pad_add_fusion.refs_0_.at, bf16[512,4096]{1,0:T(8,128)(2,1)} %refs_1_.3, bf16[1024,256]{1,0:T(8,128)(2,1)S(1)} %copy-done.5), custom_call_target="tpu_custom_call" | custom-call | flops 3449999872 | bytes 300000 | tf_op jit(solution)/shard_map/pack_weight/pallas_call | solution.py:109
  24.5 14.3 %collective-permute-done.1.g3 = bf16[1024,512]{1,0:T(8,128)(2,1)S(1)} collective-permute-done((bf16[1024,512]{1,0:T(8,128)(2,1)S(1)}, bf16[1024,512]{1,0:T(8,128)(2,1)S(1)}, u32[]{:S(2)}, u32[]{:S(2)}) %collective-permute-start.1) | collective-permute-done | bytes 1048608 | tf_op jit(solution)/shard_map/ppermute | solution.py:56
  40.7 2.7 %collective-permute-start.4 = (bf16[512,512]{1,0:T(8,128)(2,1)}, bf16[512,512]{1,0:T(8,128)(2,1)}, u32[]{:S(2)}, u32[]{:S(2)}) collective-permute-start(bf16[512,512]{1,0:T(8,128)(2,1)} %slice.105), channel_id=1, source_target_pairs={{0,6},{1,7},{2,0},{3,1},{4,2},{5,3},{6,4},{7,5},{8,14},{9,15},{10,... | collective-permute-start | bytes 1572872 | tf_op jit(solution)/shard_map/ppermute | solution.py:56
  43.4 2.2 %all-gather.3.cloned.1.call-done.refs_7_.refs_11_ = bf16[8192,256]{1,0:T(8,128)(2,1)} async-done(((bf16[1024,256]{1,0:T(8,128)(2,1)}), bf16[8192,256]{1,0:T(8,128)(2,1)}) %all-gather.3.cloned.1.call-update) | async-done | bytes 4194320 | tf_op jit(solution)/shard_map/all_gather | solution.py:502
  45.5 11.5 %attention_fwd.2 = (bf16[1024,512]{1,0:T(8,128)(2,1)}, f32[128,256]{1,0:T(8,128)}) custom-call(s32[4]{0:T(128)} %copy-done.6, s32[9]{0:T(128)} %get-tuple-element.68.refs_1_, s32[16]{0:T(128)} %get-tuple-element.55.refs_2_, s32[16]{0:T(128)} %get-tuple-element.54.refs_3_, bf16[1024,512]{1,0:T(8,128)(2,1)} %refs_4_.9, bf16[1024,128]{1,0:T(8,128)(2,1)} %refs_5_.9, ...), custom_call_target="tpu_custom_call" | custom-call | flops 344999985152 | bytes 30000000 | tf_op jit(solution)/shard_map/attention_fwd/pallas_call | solution.py:109
  58.9 2.1 collective-permute-done.6.refs_8_.refs_9_.refs_10_.refs_11_
  62.0 8.8 %grad_projection.1 = (bf16[1024,512]{1,0:T(8,128)(2,1)}, bf16[1024,512]{1,0:T(8,128)(2,1)}) custom-call(s32[4]{0:T(128)} %copy-done.6, bf16[1024,512]{1,0:T(8,128)(2,1)} %g0.1, bf16[1024,512]{1,0:T(8,128)(2,1)} %copy-done.9, bf16[512,512]{1,0:T(8,128)(2,1)} %hold.5.g2_low, bf16[512,512]{1,0:T(8,128)(2,1)} %collective-permute-done.4.refs_3_.g2_high, ...), custom_call_target="tpu_custom_call" | custom-call | flops 11500000 | bytes 1000 | tf_op jit(solution)/shard_map/grad_projection/pallas_call | solution.py:422
  72.1 18.3 %all-gather.5.cloned.1.call-done.refs_9_.refs_11_ = bf16[8192,256]{1,0:T(8,128)(2,1)} async-done(((bf16[1024,256]{1,0:T(8,128)(2,1)}), bf16[8192,256]{1,0:T(8,128)(2,1)}) %all-gather.5.cloned.1.call-update) | async-done | bytes 4194320 | tf_op jit(solution)/shard_map/all_gather | solution.py:502
  90.5 12.2 %attention_fwd.3 = (bf16[1024,512]{1,0:T(8,128)(2,1)}, f32[128,256]{1,0:T(8,128)}) custom-call(s32[4]{0:T(128)} %copy-done.6, s32[9]{0:T(128)} %get-tuple-element.69.refs_1_, s32[16]{0:T(128)} %get-tuple-element.55.refs_2_, s32[16]{0:T(128)} %get-tuple-element.54.refs_3_, bf16[1024,512]{1,0:T(8,128)(2,1)} %refs_4_.9, bf16[1024,128]{1,0:T(8,128)(2,1)} %refs_5_.9, ...), custom_call_target="tpu_custom_call" | custom-call | flops 344999985152 | bytes 30000000 | tf_op jit(solution)/shard_map/attention_fwd/pallas_call | solution.py:109
  104.2 19.6 %attention_bwd.3 = (bf16[1024,512]{1,0:T(8,128)(2,1)}, bf16[1024,128]{1,0:T(8,128)(2,1)}, bf16[1024,128]{1,0:T(8,128)(2,1)}, bf16[8192,256]{1,0:T(8,128)(2,1)}) custom-call(s32[4]{0:T(128)} %copy-done.6, s32[9]{0:T(128)} %get-tuple-element.69.refs_1_, s32[16]{0:T(128)} %get-tuple-element.55.refs_2_, s32[16]{0:T(128)} %get-tuple-element.54.refs_3_, ...), custom_call_target="tpu_custom_call" | custom-call | flops 17250000896 | bytes 1500000 | tf_op jit(solution)/shard_map/attention_bwd/pallas_call | solution.py:109
  123.7 8.3 %attention_bwd.4 = (bf16[1024,512]{1,0:T(8,128)(2,1)}, bf16[1024,128]{1,0:T(8,128)(2,1)}, bf16[1024,128]{1,0:T(8,128)(2,1)}, bf16[4096,256]{1,0:T(8,128)(2,1)}) custom-call(s32[4]{0:T(128)} %copy-done.6, s32[9]{0:T(128)} %get-tuple-element.68.refs_1_, s32[16]{0:T(128)} %get-tuple-element.55.refs_2_, s32[16]{0:T(128)} %get-tuple-element.54.refs_3_, ...), custom_call_target="tpu_custom_call" | custom-call | flops 11500000 | bytes 1000 | tf_op jit(solution)/shard_map/attention_bwd/pallas_call | solution.py:109
  132.1 3.5 %collective-permute-start.13 = (bf16[4096,256]{1,0:T(8,128)(2,1)}, bf16[4096,256]{1,0:T(8,128)(2,1)}, u32[]{:S(2)}, u32[]{:S(2)}) collective-permute-start(bf16[4096,256]{1,0:T(8,128)(2,1)} %get-tuple-element.42.refs_1_), channel_id=1, source_target_pairs={{0,8},{8,0},{16,24},{24,16},{32,40},{40,32},{48,56},{56,48},{64,72... | collective-permute-start | bytes 6291464 | tf_op jit(solution)/shard_map/ppermute | solution.py:60
  138.1 8.5 %out_projection.1 = (bf16[1024,512]{1,0:T(8,128)(2,1)}, bf16[1024,512]{1,0:T(8,128)(2,1)}, bf16[1024,512]{1,0:T(8,128)(2,1)}, bf16[1024,512]{1,0:T(8,128)(2,1)}) custom-call(s32[4]{0:T(128)} %copy-done.6, bf16[1024,512]{1,0:T(8,128)(2,1)} %get-tuple-element.35.refs_7_.att, bf16[1024,512]{1,0:T(8,128)(2,1)} %copy-done.1, bf16[512,2048]{1,0:T(8,128)(2,1)} %copy-done, ...), custom_call_target="tpu_custom_call" | custom-call | flops 11500000 | bytes 1000 | tf_op jit(solution)/shard_map/out_projection/pallas_call | solution.py:422
  146.6 2.2 %fusion.7 = (bf16[512,512]{1,0:T(8,128)(2,1)}, bf16[512,512]{1,0:T(8,128)(2,1)}) fusion(bf16[1024,512]{1,0:T(8,128)(2,1)} %get-tuple-element.45), kind=kLoop, calls=%fused_computation.63 | loop fusion | bytes 2097152 | tf_op jit(solution)/shard_map/slice | solution.py:534
  148.8 2.4 %collective-permute-start.9 = (bf16[512,512]{1,0:T(8,128)(2,1)}, bf16[512,512]{1,0:T(8,128)(2,1)}, u32[]{:S(2)}, u32[]{:S(2)}) collective-permute-start(bf16[512,512]{1,0:T(8,128)(2,1)} %get-tuple-element.64), channel_id=1, source_target_pairs={{0,6},{1,7},{2,0},{3,1},{4,2},{5,3},{6,4},{7,5},{8,14},{9,15},{10,... | collective-permute-start | bytes 1572872 | tf_op jit(solution)/shard_map/ppermute | solution.py:56
  151.2 17.9 %attention_bwd.5 = (bf16[1024,512]{1,0:T(8,128)(2,1)}, bf16[1024,128]{1,0:T(8,128)(2,1)}, bf16[1024,128]{1,0:T(8,128)(2,1)}, bf16[4096,256]{1,0:T(8,128)(2,1)}) custom-call(s32[4]{0:T(128)} %copy-done.6, s32[9]{0:T(128)} %get-tuple-element.68.refs_1_, s32[16]{0:T(128)} %get-tuple-element.55.refs_2_, s32[16]{0:T(128)} %get-tuple-element.54.refs_3_, ...), custom_call_target="tpu_custom_call" | custom-call | flops 344999985152 | bytes 30000000 | tf_op jit(solution)/shard_map/attention_bwd/pallas_call | solution.py:109
  173.3 2.3 %collective-permute-start.10 = (bf16[1024,512]{1,0:T(8,128)(2,1)}, bf16[1024,512]{1,0:T(8,128)(2,1)}, u32[]{:S(2)}, u32[]{:S(2)}) collective-permute-start(bf16[1024,512]{1,0:T(8,128)(2,1)} %pad_maximum_fusion), channel_id=1, source_target_pairs={{0,6},{1,7},{2,0},{3,1},{4,2},{5,3},{6,4},{7,5},{8,14},{9,15},{10,... | collective-permute-start | bytes 3145736 | tf_op jit(solution)/shard_map/ppermute | solution.py:56
  179.9 5.7 %collective-permute-done.16 = bf16[512,256]{1,0:T(8,128)(2,1)S(1)} collective-permute-done((bf16[512,256]{1,0:T(8,128)(2,1)S(1)}, bf16[512,256]{1,0:T(8,128)(2,1)S(1)}, u32[]{:S(2)}, u32[]{:S(2)}) %collective-permute-start.16) | collective-permute-done | bytes 262176 | tf_op jit(solution)/shard_map/ppermute | solution.py:60
  188.4 3.4 %collective-permute-start.15 = (bf16[1024,256]{1,0:T(8,128)(2,1)}, bf16[1024,256]{1,0:T(8,128)(2,1)}, u32[]{:S(2)}, u32[]{:S(2)}) collective-permute-start(bf16[1024,256]{1,0:T(8,128)(2,1)} %pad_maximum_fusion.2), channel_id=1, source_target_pairs={{0,48},{8,56},{16,0},{24,8},{32,16},{40,24},{48,32},{56,40},{64,11... | collective-permute-start | bytes 1572872 | tf_op jit(solution)/shard_map/ppermute | solution.py:60
  191.8 3.6 %collective-permute-done.12 = bf16[1024,512]{1,0:T(8,128)(2,1)} collective-permute-done((bf16[1024,512]{1,0:T(8,128)(2,1)S(1)}, bf16[1024,512]{1,0:T(8,128)(2,1)}, u32[]{:S(2)}, u32[]{:S(2)}) %collective-permute-start.12) | collective-permute-done | bytes 1048608 | tf_op jit(solution)/shard_map/ppermute | solution.py:56
  197.4 3.2 %add_convert_fusion = bf16[1024,512]{1,0:T(8,128)(2,1)} fusion(bf16[1024,512]{1,0:T(8,128)(2,1)} %collective-permute-done.12, bf16[1024,512]{1,0:T(8,128)(2,1)} %collective-permute-done.10, bf16[1024,512]{1,0:T(8,128)(2,1)} %get-tuple-element.43), kind=kLoop, calls=%fused_computation | loop fusion | flops 3145728 | bytes 4194304 | tf_op jit(solution)/shard_map/convert_element_type | solution.py:467
  200.6 2.0 collective-permute-done.17
  202.6 3.1 %collective-permute-done.18 = bf16[1024,256]{1,0:T(8,128)(2,1)S(1)} collective-permute-done((bf16[1024,256]{1,0:T(8,128)(2,1)}, bf16[1024,256]{1,0:T(8,128)(2,1)S(1)}, u32[]{:S(2)}, u32[]{:S(2)}) %collective-permute-start.18) | collective-permute-done | bytes 524320 | tf_op jit(solution)/shard_map/ppermute | solution.py:60
  (91 shorter events, 35.3 us)
Async XLA Ops:
  7.2 38.3 %all-gather.3.cloned.1.call-start = ((), (), s32[]{:S(2)}) async-start(), calls=%async_computation.1 | async-start | bytes 4718592 | tf_op jit(solution)/shard_map/all_gather | solution.py:502
  9.2 81.2 %all-gather.5.cloned.1.call-start = ((), (), s32[]{:S(2)}) async-start(), calls=%async_computation.2 | async-start | bytes 4718592 | tf_op jit(solution)/shard_map/all_gather | solution.py:502
  9.3 47.8 %collective-permute-start = (bf16[1024,256]{1,0:T(8,128)(2,1)}, bf16[1024,256]{1,0:T(8,128)(2,1)}, u32[]{:S(2)}, u32[]{:S(2)}) collective-permute-start(bf16[1024,256]{1,0:T(8,128)(2,1)} %pack_prompts.1.refs_2_), channel_id=1, source_target_pairs={{0,64},{8,72},{16,80},{24,88},{32,96},{40,104},{48,112},{56,120},{... | collective-permute-start | bytes 1572872 | tf_op jit(solution)/shard_map/ppermute | solution.py:60
  13.8 25.0 %collective-permute-start.1 = (bf16[1024,512]{1,0:T(8,128)(2,1)S(1)}, bf16[1024,512]{1,0:T(8,128)(2,1)S(1)}, u32[]{:S(2)}, u32[]{:S(2)}) collective-permute-start(bf16[1024,512]{1,0:T(8,128)(2,1)S(1)} %copy-done.11), channel_id=1, source_target_pairs={{0,2},{1,3},{2,4},{3,5},{4,6},{5,7},{6,0},{7,1},{8,10},{9,11},{10,... | collective-permute-start | bytes 3145736 | tf_op jit(solution)/shard_map/ppermute | solution.py:56
  15.0 24.8 %collective-permute-start.3 = (bf16[1024,512]{1,0:T(8,128)(2,1)S(1)}, bf16[1024,512]{1,0:T(8,128)(2,1)S(1)}, u32[]{:S(2)}, u32[]{:S(2)}) collective-permute-start(bf16[1024,512]{1,0:T(8,128)(2,1)S(1)} %copy-done.11), channel_id=1, source_target_pairs={{0,6},{1,7},{2,0},{3,1},{4,2},{5,3},{6,4},{7,5},{8,14},{9,15},{10,... | collective-permute-start | bytes 3145736 | tf_op jit(solution)/shard_map/ppermute | solution.py:56
  22.2 34.9 %collective-permute-start.5 = (bf16[256,2048]{1,0:T(8,128)(2,1)}, bf16[256,2048]{1,0:T(8,128)(2,1)}, u32[]{:S(2)}, u32[]{:S(2)}) collective-permute-start(bf16[256,2048]{1,0:T(8,128)(2,1)} %get-tuple-element.32), channel_id=1, source_target_pairs={{0,1},{1,0},{2,3},{3,2},{4,5},{5,4},{6,7},{7,6},{8,9},{9,8},{10,11... | collective-permute-start | bytes 3145736 | tf_op jit(solution)/shard_map/ppermute | solution.py:56
  38.8 18.2 %copy-start.8 = (bf16[1024,512]{1,0:T(8,128)(2,1)}, bf16[1024,512]{1,0:T(8,128)(2,1)S(1)}, u32[]{:S(2)}) copy-start(bf16[1024,512]{1,0:T(8,128)(2,1)S(1)} %collective-permute-done.1.g3) | copy-start | bytes 3145732
  39.8 17.3 %collective-permute-start.2 = (bf16[512,512]{1,0:T(8,128)(2,1)}, bf16[512,512]{1,0:T(8,128)(2,1)}, u32[]{:S(2)}, u32[]{:S(2)}) collective-permute-start(bf16[512,512]{1,0:T(8,128)(2,1)} %slice.104), channel_id=1, source_target_pairs={{0,2},{1,3},{2,4},{3,5},{4,6},{5,7},{6,0},{7,1},{8,10},{9,11},{10,... | collective-permute-start | bytes 1572872 | tf_op jit(solution)/shard_map/ppermute | solution.py:56
  40.7 16.4 %collective-permute-start.4 = (bf16[512,512]{1,0:T(8,128)(2,1)}, bf16[512,512]{1,0:T(8,128)(2,1)}, u32[]{:S(2)}, u32[]{:S(2)}) collective-permute-start(bf16[512,512]{1,0:T(8,128)(2,1)} %slice.105), channel_id=1, source_target_pairs={{0,6},{1,7},{2,0},{3,1},{4,2},{5,3},{6,4},{7,5},{8,14},{9,15},{10,... | collective-permute-start | bytes 1572872 | tf_op jit(solution)/shard_map/ppermute | solution.py:56
  58.0 133.8 %reduce-scatter.2.cloned.1.call-start = ((), (), s32[]{:S(2)}) async-start(), calls=%async_computation.3 | async-start | bytes 4718592 | tf_op jit(solution)/shard_map/reduce_scatter | solution.py:529
  58.1 3.0 %collective-permute-start.6 = (bf16[256,2048]{1,0:T(8,128)(2,1)}, bf16[256,2048]{1,0:T(8,128)(2,1)S(1)}, u32[]{:S(2)}, u32[]{:S(2)}) collective-permute-start(bf16[256,2048]{1,0:T(8,128)(2,1)} %collective-permute-done.5.refs_4_.refs_5_.refs_6_.refs_7_), channel_id=1, source_target_pairs={{0,8},{8,0},{16,24},{24,16},{32,40},{40,32},{48,56},{56,48},{64,72... | collective-permute-start | bytes 3145736 | tf_op jit(solution)/shard_map/ppermute | solution.py:60
  70.8 33.4 %collective-permute-start.8 = (bf16[1024,512]{1,0:T(8,128)(2,1)}, bf16[1024,512]{1,0:T(8,128)(2,1)}, u32[]{:S(2)}, u32[]{:S(2)}) collective-permute-start(bf16[1024,512]{1,0:T(8,128)(2,1)} %get-tuple-element.34.refs_10_), channel_id=1, source_target_pairs={{0,1},{1,0},{2,3},{3,2},{4,5},{5,4},{6,7},{7,6},{8,9},{9,8},{10,11... | collective-permute-start | bytes 3145736 | tf_op jit(solution)/shard_map/ppermute | solution.py:56
  102.6 32.9 %collective-permute-start.7 = (bf16[1024,512]{1,0:T(8,128)(2,1)}, bf16[1024,512]{1,0:T(8,128)(2,1)S(1)}, u32[]{:S(2)}, u32[]{:S(2)}) collective-permute-start(bf16[1024,512]{1,0:T(8,128)(2,1)} %get-tuple-element.35.refs_7_.att), channel_id=1, source_target_pairs={{0,1},{1,0},{2,3},{3,2},{4,5},{5,4},{6,7},{7,6},{8,9},{9,8},{10,11... | collective-permute-start | bytes 3145736 | tf_op jit(solution)/shard_map/ppermute | solution.py:56
  132.1 43.6 %collective-permute-start.13 = (bf16[4096,256]{1,0:T(8,128)(2,1)}, bf16[4096,256]{1,0:T(8,128)(2,1)}, u32[]{:S(2)}, u32[]{:S(2)}) collective-permute-start(bf16[4096,256]{1,0:T(8,128)(2,1)} %get-tuple-element.42.refs_1_), channel_id=1, source_target_pairs={{0,8},{8,0},{16,24},{24,16},{32,40},{40,32},{48,56},{56,48},{64,72... | collective-permute-start | bytes 6291464 | tf_op jit(solution)/shard_map/ppermute | solution.py:60
  148.8 22.1 %collective-permute-start.9 = (bf16[512,512]{1,0:T(8,128)(2,1)}, bf16[512,512]{1,0:T(8,128)(2,1)}, u32[]{:S(2)}, u32[]{:S(2)}) collective-permute-start(bf16[512,512]{1,0:T(8,128)(2,1)} %get-tuple-element.64), channel_id=1, source_target_pairs={{0,6},{1,7},{2,0},{3,1},{4,2},{5,3},{6,4},{7,5},{8,14},{9,15},{10,... | collective-permute-start | bytes 1572872 | tf_op jit(solution)/shard_map/ppermute | solution.py:56
  151.2 18.0 %collective-permute-start.11 = (bf16[512,512]{1,0:T(8,128)(2,1)}, bf16[512,512]{1,0:T(8,128)(2,1)}, u32[]{:S(2)}, u32[]{:S(2)}) collective-permute-start(bf16[512,512]{1,0:T(8,128)(2,1)} %get-tuple-element.65), channel_id=1, source_target_pairs={{0,2},{1,3},{2,4},{3,5},{4,6},{5,7},{6,0},{7,1},{8,10},{9,11},{10,... | collective-permute-start | bytes 1572872 | tf_op jit(solution)/shard_map/ppermute | solution.py:56
  151.2 18.0 %copy-start.13 = (bf16[1024,512]{1,0:T(8,128)(2,1)S(1)}, bf16[1024,512]{1,0:T(8,128)(2,1)}, u32[]{:S(2)}) copy-start(bf16[1024,512]{1,0:T(8,128)(2,1)} %get-tuple-element.46) | copy-start | bytes 3145732
  170.6 24.8 %collective-permute-start.12 = (bf16[1024,512]{1,0:T(8,128)(2,1)S(1)}, bf16[1024,512]{1,0:T(8,128)(2,1)}, u32[]{:S(2)}, u32[]{:S(2)}) collective-permute-start(bf16[1024,512]{1,0:T(8,128)(2,1)S(1)} %pad_maximum_fusion.1), channel_id=1, source_target_pairs={{0,2},{1,3},{2,4},{3,5},{4,6},{5,7},{6,0},{7,1},{8,10},{9,11},{10,... | collective-permute-start | bytes 3145736 | tf_op jit(solution)/shard_map/ppermute | solution.py:56
  173.3 24.1 %collective-permute-start.10 = (bf16[1024,512]{1,0:T(8,128)(2,1)}, bf16[1024,512]{1,0:T(8,128)(2,1)}, u32[]{:S(2)}, u32[]{:S(2)}) collective-permute-start(bf16[1024,512]{1,0:T(8,128)(2,1)} %pad_maximum_fusion), channel_id=1, source_target_pairs={{0,6},{1,7},{2,0},{3,1},{4,2},{5,3},{6,4},{7,5},{8,14},{9,15},{10,... | collective-permute-start | bytes 3145736 | tf_op jit(solution)/shard_map/ppermute | solution.py:56
  177.1 8.4 %collective-permute-start.16 = (bf16[512,256]{1,0:T(8,128)(2,1)S(1)}, bf16[512,256]{1,0:T(8,128)(2,1)S(1)}, u32[]{:S(2)}, u32[]{:S(2)}) collective-permute-start(bf16[512,256]{1,0:T(8,128)(2,1)S(1)} %hold.7), channel_id=1, source_target_pairs={{0,16},{8,24},{16,32},{24,40},{32,48},{40,56},{48,0},{56,8},{64,80... | collective-permute-start | bytes 786440 | tf_op jit(solution)/shard_map/ppermute | solution.py:60
  177.9 7.6 %collective-permute-start.14 = (bf16[512,256]{1,0:T(8,128)(2,1)S(1)}, bf16[512,256]{1,0:T(8,128)(2,1)S(1)}, u32[]{:S(2)}, u32[]{:S(2)}) collective-permute-start(bf16[512,256]{1,0:T(8,128)(2,1)S(1)} %get-tuple-element.61), channel_id=1, source_target_pairs={{0,48},{8,56},{16,0},{24,8},{32,16},{40,24},{48,32},{56,40},{64,11... | collective-permute-start | bytes 786440 | tf_op jit(solution)/shard_map/ppermute | solution.py:60
  187.6 15.0 %collective-permute-start.17 = (bf16[1024,256]{1,0:T(8,128)(2,1)}, bf16[1024,256]{1,0:T(8,128)(2,1)}, u32[]{:S(2)}, u32[]{:S(2)}) collective-permute-start(bf16[1024,256]{1,0:T(8,128)(2,1)} %pad_maximum_fusion.3), channel_id=1, source_target_pairs={{0,16},{8,24},{16,32},{24,40},{32,48},{40,56},{48,0},{56,8},{64,80... | collective-permute-start | bytes 1572872 | tf_op jit(solution)/shard_map/ppermute | solution.py:60
  188.4 14.2 %collective-permute-start.15 = (bf16[1024,256]{1,0:T(8,128)(2,1)}, bf16[1024,256]{1,0:T(8,128)(2,1)}, u32[]{:S(2)}, u32[]{:S(2)}) collective-permute-start(bf16[1024,256]{1,0:T(8,128)(2,1)} %pad_maximum_fusion.2), channel_id=1, source_target_pairs={{0,48},{8,56},{16,0},{24,8},{32,16},{40,24},{48,32},{56,40},{64,11... | collective-permute-start | bytes 1572872 | tf_op jit(solution)/shard_map/ppermute | solution.py:60
  191.8 13.9 %collective-permute-start.18 = (bf16[1024,256]{1,0:T(8,128)(2,1)}, bf16[1024,256]{1,0:T(8,128)(2,1)S(1)}, u32[]{:S(2)}, u32[]{:S(2)}) collective-permute-start(bf16[1024,256]{1,0:T(8,128)(2,1)} %reduce-scatter.2.cloned.1.call-done), channel_id=1, source_target_pairs={{0,64},{8,72},{16,80},{24,88},{32,96},{40,104},{48,112},{56,120},{... | collective-permute-start | bytes 1572872 | tf_op jit(solution)/shard_map/ppermute | solution.py:60
  (14 other events, 68.6 us)
Sparse Core Ops, SparseCore 0:
  9.7 35.7 all-gather.2
  58.1 32.2 all-gather.4
  123.9 36.8 reduce-scatter.1
